TPU v7x, 32 devices: a whole 2x2x4 slice. The times are simulated.
32 devices in a mesh: seq: 8 (over z, y), head: 4 (over x, core).
Axes of the slice: x: 2, y: 2, z: 4, core: 2. Of those that a mesh axis runs over, the one named last changes fastest.
Arguments:
- queries: bfloat16 [8192, 4096], P('seq', 'head'), may hold values from -6 to 6
- keys: bfloat16 [8192, 4096], P('seq', 'head'), may hold values from -6 to 6
- values: bfloat16 [8192, 4096], P('seq', 'head'), may hold values from -6 to 6
- decay: float32 [8192, 4096], P('seq', 'head'), as said below
- beta: float32 [32, 8192], P('head', 'seq'), may hold values from 0.002 to 0.98
- wy_inverse: float32 [128, 64, 2048], P('seq', None, 'head')
- out_gate: bfloat16 [8192, 4096], P('seq', 'head'), may hold values from -6 to 6
- norm_gain: float32 [128], replicated, may hold values from 0.1 to 1.9
- out_proj: bfloat16 [4096, 2304], P('head'), may hold values from -0.125 to 0.125
- grad_out: bfloat16 [8192, 2304], P('seq', 'head'), may hold values from -6 to 6
- resets: int32 [8], P('seq'), may hold values from 0 to 16, as said below
Outputs:
- grad_queries: bfloat16 [8192, 4096], P('seq', 'head')
- grad_keys: bfloat16 [8192, 4096], P('seq', 'head')
- grad_values: bfloat16 [8192, 4096], P('seq', 'head')
- grad_decay: float32 [8192, 4096], P('seq', 'head')
- grad_beta: float32 [32, 8192], P('head', 'seq')
- grad_gate: bfloat16 [8192, 4096], P('seq', 'head')
Inputs may be any that keep to these rules, and one draw needn't show every extreme that they name: `resets`: 16 means that no document starts in that index of seq; the first value is 0 and the last is 16. Natural logarithms of decay factors, at most 0.
All inputs are finite; a program needn't handle non-finite values.
Results may differ from a plain program's by a relative error of at most 0.02.
Values may be sent and summed in bfloat16 or wider, within the bound.
A program may use at most 192 MiB of HBM per device.

v0:
```python
import jax
import jax.numpy as jnp
from jax import lax
from jax.sharding import PartitionSpec as P

DK = 128
DV = 128
GROUP = 64


precise = lax.Precision.HIGHEST


def from_behind(x, axis, by):
    devices = lax.axis_size(axis)
    pairs = [(i, i + by) for i in range(devices) if 0 <= i + by < devices]
    return lax.ppermute(x, axis, pairs)


def to_blocks(array, heads, width):
    count = array.shape[0] // GROUP
    return array.reshape(count, GROUP, heads, width).transpose(0, 2, 1, 3)


def from_blocks(array):
    count, heads, length, width = array.shape
    return array.transpose(0, 2, 1, 3).reshape(count * length, heads * width)


def unit_rows(array, width, multiplier_term):
    rows = array.reshape(array.shape[0], -1, width)
    scale = lax.rsqrt(jnp.sum(rows * rows, axis=-1, keepdims=True) + 1e-06)
    return (rows * scale * multiplier_term).reshape(array.shape)


def low_product(form, left, right):
    return jnp.einsum(
        form,
        left.astype(jnp.bfloat16),
        right.astype(jnp.bfloat16),
        preferred_element_type=jnp.float32,
    )


def group_step(state, block):
    query_rows, key_rows, value_rows, gate_rows, beta_rows, wy_rows, keep_flag = block
    entry = state * keep_flag
    cumul = jnp.cumsum(gate_rows, axis=1)
    final = cumul[:, -1:, :]
    query_dec = query_rows * jnp.exp(cumul)
    key_dec = key_rows * jnp.exp(cumul)
    key_inv = key_rows * jnp.exp(-cumul)
    key_tail = key_rows * jnp.exp(final - cumul)
    lower = jnp.tril(jnp.ones((GROUP, GROUP), jnp.float32))
    predicted = jnp.einsum("hld,hdv->hlv", key_dec, entry, precision=precise)
    target = beta_rows[:, :, None] * (value_rows - predicted)
    update = low_product("hij,hjv->hiv", wy_rows, target)
    scores = low_product("hid,hjd->hij", query_dec, key_inv) * lower
    output = jnp.einsum("hld,hdv->hlv", query_dec, entry, precision=precise)
    output = output + low_product("hij,hjv->hiv", scores, update)
    carried = jnp.exp(final[:, 0, :])[:, :, None] * entry
    carried = carried + low_product("hld,hlv->hdv", key_tail, update)
    return (carried, output)


def core(query_unit, key_unit, value_f, decay, beta, wy_inverse, keep, state):
    heads = beta.shape[0]
    count = query_unit.shape[0] // GROUP
    blocks = (
        to_blocks(query_unit, heads, DK),
        to_blocks(key_unit, heads, DK),
        to_blocks(value_f, heads, DV),
        to_blocks(decay, heads, DK),
        beta.reshape(heads, count, GROUP).transpose(1, 0, 2),
        wy_inverse.reshape(count, GROUP, heads, GROUP).transpose(0, 2, 1, 3),
        keep,
    )
    final, outputs = lax.scan(jax.checkpoint(group_step), state, blocks)
    return (from_blocks(outputs), final)


def transition(key_unit, decay, beta, wy_inverse, keep):
    heads = beta.shape[0]
    count = key_unit.shape[0] // GROUP
    blocks = (
        to_blocks(key_unit, heads, DK),
        to_blocks(decay, heads, DK),
        beta.reshape(heads, count, GROUP).transpose(1, 0, 2),
        wy_inverse.reshape(count, GROUP, heads, GROUP).transpose(0, 2, 1, 3),
        keep,
    )
    identity = jnp.broadcast_to(jnp.eye(DK, dtype=jnp.float32), (heads, DK, DK))

    def advance(total, block):
        key_rows, gate_rows, beta_rows, wy_rows, keep_flag = block
        cumul = jnp.cumsum(gate_rows, axis=1)
        final = cumul[:, -1:, :]
        key_dec = key_rows * jnp.exp(cumul)
        key_tail = key_rows * jnp.exp(final - cumul)
        mixed = jnp.einsum(
            "hij,hjd->hid", wy_rows, beta_rows[:, :, None] * key_dec, precision=precise
        )
        matrix = identity * jnp.exp(final[:, 0, :])[:, :, None]
        matrix = (
            matrix - jnp.einsum("hld,hle->hde", key_tail, mixed, precision=precise)
        ) * keep_flag
        return (jnp.einsum("hij,hjk->hik", matrix, total, precision=precise), None)

    product, _ = lax.scan(advance, identity, blocks)
    return product


def gated_norm(output, gate, gain):
    rows = output.reshape(output.shape[0], -1, DV)
    scale = lax.rsqrt(jnp.mean(rows * rows, axis=-1, keepdims=True) + 1e-06)
    gates = jax.nn.sigmoid(gate.reshape(rows.shape))
    return (rows * scale * gain * gates).reshape(output.shape)


def apply_map(matrix, state):
    return jnp.einsum("hij,hjk->hik", matrix, state, precision=precise)


def per_device(
    queries, keys, values, decay, beta, wy_inverse, out_gate, norm_gain, out_proj, grad_out, resets
):
    tokens_here = queries.shape[0]
    heads = beta.shape[0]
    count = tokens_here // GROUP
    upstream = lax.dot_general(
        lax.all_gather(grad_out, "head", axis=1, tiled=True),
        out_proj,
        (((1,), (1,)), ((), ())),
        preferred_element_type=jnp.float32,
    )
    keep = (jnp.arange(count) != resets[0]).astype(jnp.float32)
    query_f = queries.astype(jnp.float32)
    key_f = keys.astype(jnp.float32)
    value_f = values.astype(jnp.float32)
    gate_f = out_gate.astype(jnp.float32)

    def normalize(query_in, key_in):
        return (unit_rows(query_in, DK, DK ** (-0.5)), unit_rows(key_in, DK, 1.0))

    (query_unit, key_unit), unit_pull = jax.vjp(normalize, query_f, key_f)
    empty = jnp.zeros((heads, DK, DV), jnp.float32)
    _, offset = core(query_unit, key_unit, value_f, decay, beta, wy_inverse, keep, empty)
    summary = transition(key_unit, decay, beta, wy_inverse, keep)

    def relay_forward(turn, carry):
        incoming = from_behind(carry[1].astype(jnp.bfloat16), "seq", 1).astype(jnp.float32)
        return (incoming, apply_map(summary, incoming) + offset)

    state_in, _ = lax.fori_loop(0, lax.axis_size("seq"), relay_forward, (empty, offset))

    def layer(query_in, key_in, value_in, gate_log, beta_in, gate_in, state):
        output, final = core(query_in, key_in, value_in, gate_log, beta_in, wy_inverse, keep, state)
        return (gated_norm(output, gate_in, norm_gain), final)

    (normed, final), pullback = jax.vjp(
        layer, query_unit, key_unit, value_f, decay, beta, gate_f, state_in
    )
    first = pullback((upstream, jnp.zeros_like(final)))
    residual = first[6]
    flipped = summary.transpose(0, 2, 1)

    def relay_back(turn, carry):
        incoming = from_behind(carry[1].astype(jnp.bfloat16), "seq", -1).astype(jnp.float32)
        return (incoming, apply_map(flipped, incoming) + residual)

    state_grad, _ = lax.fori_loop(0, lax.axis_size("seq"), relay_back, (empty, residual))
    second = pullback((jnp.zeros_like(normed), state_grad))
    totals = [first[slot] + second[slot] for slot in range(6)]
    grad_query, grad_key = unit_pull((totals[0], totals[1]))
    return (
        grad_query.astype(jnp.bfloat16),
        grad_key.astype(jnp.bfloat16),
        totals[2].astype(jnp.bfloat16),
        totals[3],
        totals[4],
        totals[5].astype(jnp.bfloat16),
    )


def solution(mesh):
    return jax.shard_map(
        per_device,
        mesh=mesh,
        in_specs=(
            P("seq", "head"),
            P("seq", "head"),
            P("seq", "head"),
            P("seq", "head"),
            P("head", "seq"),
            P("seq", None, "head"),
            P("seq", "head"),
            P(),
            P("head", None),
            P("seq", "head"),
            P("seq"),
        ),
        out_specs=(
            P("seq", "head"),
            P("seq", "head"),
            P("seq", "head"),
            P("seq", "head"),
            P("head", "seq"),
            P("seq", "head"),
        ),
        check_vma=False,
    )
```

profile of v0, /device:TPU:0, one launch (start us, length us, event | category | flops | bytes accessed | tf_op | source)
XLA Modules:
  0.0 1893.0 jit_solution(266594859557866176)
XLA Ops:
  19.5 7.9 fusion.149
  55.8 133.8 %while.115 = (s32[]{:T(128)}, f32[8,128,128]{2,1,0:T(8,128)S(1)}, f32[16,8,64,128]{3,1,2,0:T(8,128)}, f32[16]{0:T(128)}, f32[16,8,64,128]{3,1,2,0:T(8,128)}, /*i...) while((s32[]{:T(128)}, f32[8,128,128]{2,1,0:T(8,128)S(1)}, ...), condition=%wide.region_3.4_spmd.clone, body=%wide.region_1.3_spmd.clone.sunk | while | flops 131268608 | bytes 4095628 | solution.py:78
  189.8 115.4 %while.113 = (s32[]{:T(128)}, f32[8,128,128]{2,1,0:T(8,128)S(1)}, f32[16,8,64,128]{3,1,2,0:T(8,128)}, f32[16,8,64,128]{3,1,2,0:T(8,128)}, f32[16,8,64,64]{3,2,1,...) while((s32[]{:T(128)}, f32[8,128,128]{2,1,0:T(8,128)S(1)}, ...), condition=%wide.region_6.7_spmd.clone, body=%wide.region_4.6_spmd.clone.sunk | while | flops 357105664 | bytes 6130805 | solution.py:109
  306.0 84.5 %while.110 = (s32[]{:T(128)}, f32[8,128,128]{2,1,0:T(8,128)}, bf16[8,128,128]{2,1,0:T(8,128)(2,1)S(1)}, f32[8,128,128]{2,1,0:T(8,128)S(1)}, f32[8,128,128]{2,1,0:T(8,128)S(1)}, /*index=5*/s32[]{:T(128)}) while((s32[]{:T(128)}, f32[8,128,128]{2,1,0:T(8,128)}, bf16[8,128,128]{2,1,0:T(8,128)(2,1)S(1)}, f32[8,128,128]{2,1,0:T(8,128)S(1)}, ...), condition=%wide.region_8.9_spmd, body=%wide.region_7.8_spmd.sunk | while | flops 201719808 | bytes 3407981 | solution.py:154
  393.1 200.7 %while.114 = (s32[]{:T(128)}, f32[8,128,128]{2,1,0:T(8,128)S(1)}, f32[16,8,64,128]{3,2,1,0:T(8,128)}, f32[16,8,128,128]{3,2,1,0:T(8,128)}, f32[16,8,64,128]{3,1,...) while((s32[]{:T(128)}, f32[8,128,128]{2,1,0:T(8,128)S(1)}, ...), condition=%wide.region_12.13_spmd.clone, body=%wide.region_10.12_spmd.clone.sunk | while | flops 249044992 | bytes 8716445 | solution.py:78
  606.9 8.8 fusion.170
  626.9 11.2 fusion.140
  648.7 524.7 %while.116 = (s32[]{:T(128)}, f32[8,128,128]{2,1,0:T(8,128)S(1)}, f32[16,8,64,128]{3,1,2,0:T(8,128)}, f32[16,8,64,128]{3,1,2,0:T(8,128)}, f32[16,8,64,128]{3,2,1...) while((s32[]{:T(128)}, f32[8,128,128]{2,1,0:T(8,128)S(1)}, ...), condition=%wide.region_21.22_spmd.clone, body=%wide.region_15.21_spmd.clone.sunk | while | flops 609197568 | bytes 25559316 | solution.py:78
  690.5 6.3 fusion.425
  723.3 6.3 fusion.425
  756.1 6.3 fusion.425
  821.7 6.3 fusion.425
  854.5 6.3 fusion.425
  887.2 6.3 fusion.425
  1174.3 99.2 %while.111 = (s32[]{:T(128)}, f32[8,128,128]{2,1,0:T(8,128)}, bf16[8,128,128]{2,1,0:T(8,128)(2,1)S(1)}, f32[8,128,128]{2,1,0:T(8,128)}, f32[8,128,128]{2,1,0:T(8,128)S(1)}, /*index=5*/s32[]{:T(128)}) while((s32[]{:T(128)}, f32[8,128,128]{2,1,0:T(8,128)}, bf16[8,128,128]{2,1,0:T(8,128)(2,1)S(1)}, f32[8,128,128]{2,1,0:T(8,128)}, ...), condition=%wide.region_23.24_spmd, body=%wide.region_22.23_spmd.sunk | while | flops 201719808 | bytes 3407981 | solution.py:171
  1175.6 9.6 collective-permute-done.1
  1188.8 11.8 collective-permute-done.1
  1204.1 9.5 collective-permute-done.1
  1217.2 8.6 collective-permute-done.1
  1229.3 7.7 collective-permute-done.1
  1240.6 7.8 collective-permute-done.1
  1251.9 7.9 collective-permute-done.1
  1263.3 7.9 collective-permute-done.1
  1283.9 548.2 %while.112 = (s32[]{:T(128)}, f32[8,128,128]{2,1,0:T(8,128)S(1)}, f32[16,8,64,128]{3,1,2,0:T(8,128)}, f32[16,8,64,128]{3,1,2,0:T(8,128)}, f32[16,8,64,128]{3,2,1...) while((s32[]{:T(128)}, f32[8,128,128]{2,1,0:T(8,128)S(1)}, ...), condition=%wide.region_31.32_spmd, body=%wide.region_25.31_spmd.sunk | while | flops 609066496 | bytes 25559324 | solution.py:78
  (1846 shorter events, 1732.1 us)
Async XLA Ops:
  7.2 599.7 %all-gather.2.cloned.1.call-start = ((), (), s32[]{:S(2)}) async-start(), calls=%async_computation | async-start | bytes 5898240 | tf_op jit(solution)/shard_map/all_gather | solution.py:131
  19.3 8.0 copy-start.35
  306.0 10.5 collective-permute-start
  317.7 8.8 collective-permute-start
  327.8 8.4 collective-permute-start
  337.5 9.2 collective-permute-start
  347.9 9.2 collective-permute-start
  358.2 9.2 collective-permute-start
  368.6 9.9 collective-permute-start
  379.8 9.5 collective-permute-start
  600.5 6.3 copy-start.38
  615.7 6.5 copy-start.10
  617.9 8.0 copy-start.11
  1174.3 10.9 collective-permute-start.1
  1187.5 13.1 collective-permute-start.1
  1202.8 10.8 collective-permute-start.1
  1215.9 9.9 collective-permute-start.1
  1228.0 9.0 collective-permute-start.1
  1239.3 9.1 collective-permute-start.1
  1250.6 9.2 collective-permute-start.1
  1262.0 9.2 collective-permute-start.1
  1278.4 5.5 copy-start.1
  1852.7 6.3 copy-start.5
  1866.6 7.0 copy-start.29
  (47 other events, 114.7 us)
Sparse Core Ops, SparseCore 0:
  9.6 40.1 all-gather.1
where the time goes:
time: 1920 us; the launch traced here: 1890 us
  matrix products  695 us (36%)
  local copies, waits for them, and re-layouts  554 us (29%)
  other arithmetic  463 us (24%)
  waiting for transfers between devices  105 us (5%)
  starting transfers between devices  51.3 us (3%)
    another operation x96, other arithmetic, group_step(): cumul = jnp.cumsum(gate_rows, axis=1)  267 us
    dot_general x128, matrix products, group_step(): predicted = jnp.einsum('hld,hdv->hlv', key_dec, entry, precision=precise)  261 us
    squeeze x256, local copies, waits for them, and re-layouts, core(): final, outputs = lax.scan(jax.checkpoint(group_step), state, blocks)  242 us
    dot_general x320, matrix products, low_product(): jnp.einsum(form, left.astype(jnp.bfloat16), right.astype(jnp.bfloat16), p...  240 us
    dynamic_slice x128, local copies, waits for them, and re-layouts, core(): final, outputs = lax.scan(jax.checkpoint(group_step), state, blocks)  113 us
    dot_general x80, matrix products, group_step(): output = jnp.einsum('hld,hdv->hlv', query_dec, entry, precision=precise)  112 us
    ppermute x16, waiting for transfers between devices, from_behind(): return lax.ppermute(x, axis, pairs)  104 us
    dynamic_update_slice x80, local copies, waits for them, and re-layouts, core(): final, outputs = lax.scan(jax.checkpoint(group_step), state, blocks)  68.4 us
  transfers between devices with their start and end apart: 17, of which 16 were waited for; matrix products, arithmetic and copies ran while one was open for 27% of the time, Pallas kernels for 0%

commit v1 on v0

v1 whole, which is shorter than its diff:
```python
import functools

import jax
import jax.numpy as jnp
from jax import lax
from jax.experimental import pallas as pl
from jax.experimental.pallas import tpu as pltpu
from jax.sharding import PartitionSpec as P

DK = 128
DV = 128
GROUP = 64
SCALE = DK ** (-0.5)
MESH = pl.DeviceIdType.MESH
VMEM_LIMIT = 48 * 1024 * 1024
f32 = jnp.float32
bf16 = jnp.bfloat16


def nn(a, b):
    return lax.dot_general(
        a.astype(bf16), b.astype(bf16), (((1,), (0,)), ((), ())), preferred_element_type=f32
    )


def nt(a, b):
    return lax.dot_general(
        a.astype(bf16), b.astype(bf16), (((1,), (1,)), ((), ())), preferred_element_type=f32
    )


def tn(a, b):
    return lax.dot_general(
        a.astype(bf16), b.astype(bf16), (((0,), (0,)), ((), ())), preferred_element_type=f32
    )


def triangle(upper, copies):
    rows = lax.broadcasted_iota(jnp.int32, (GROUP, GROUP), 0)
    cols = lax.broadcasted_iota(jnp.int32, (GROUP, GROUP), 1)
    keep = (cols >= rows) if upper else (cols <= rows)
    one = keep.astype(f32).astype(bf16)
    return jnp.concatenate([one] * copies, axis=1)


def lower_only(x):
    rows = lax.broadcasted_iota(jnp.int32, x.shape, 0)
    cols = lax.broadcasted_iota(jnp.int32, x.shape, 1)
    return jnp.where(cols <= rows, x, 0.0)


def split_rows(x, parts):
    out = []
    for _ in range(parts):
        piece = x.astype(bf16)
        out.append(piece)
        x = x - piece.astype(f32)
    return jnp.concatenate(out, axis=0)


def cumulative(decay):
    return nn(triangle(False, 3), split_rows(decay, 3))


def unit(x):
    scale = lax.rsqrt(jnp.sum(x * x, axis=-1, keepdims=True) + 1e-06)
    return x * scale, scale


def local_kernel(
    heads, together, resets, q_ref, k_ref, v_ref, g_ref, b_ref, w_ref,
    out_ref, map_ref, enter_ref, total_ref, state,
):
    step = pl.program_id(0)

    @pl.when(step == 0)
    def _():
        eye = (
            lax.broadcasted_iota(jnp.int32, (DK, DK), 0)
            == lax.broadcasted_iota(jnp.int32, (DK, DK), 1)
        ).astype(f32)
        for h in range(heads):
            state[h, :DV] = jnp.zeros((DV, DK), f32)
            state[h, DV:] = eye

    keep = jnp.where(step == resets[0], 0.0, 1.0)
    cumul = cumulative(g_ref[...])
    grow = jnp.exp(cumul)
    shrink = jnp.exp(-cumul)
    for first in range(0, heads, together):
        hs = list(range(first, first + together))
        cols = {h: slice(h * DK, (h + 1) * DK) for h in hs}
        entry, both, inv, tail, low, pred, scores, target, update = ({} for _ in range(9))
        for h in hs:
            entry[h] = state[h] * keep
            enter_ref[0, h] = entry[h].astype(bf16)
            qu = unit(q_ref[:, cols[h]].astype(f32))[0] * SCALE
            ku = unit(k_ref[:, cols[h]].astype(f32))[0]
            up = grow[:, cols[h]]
            both[h] = jnp.concatenate([(ku * up).astype(bf16), (qu * up).astype(bf16)], axis=0)
            ki = ku * shrink[:, cols[h]]
            inv[h] = ki.astype(bf16)
            tail[h] = (ki * up[GROUP - 1 :]).astype(bf16)
        for h in hs:
            pred[h] = nt(both[h], entry[h])
            scores[h] = lower_only(nt(both[h][GROUP:], inv[h]))
        for h in hs:
            beta = b_ref[:, h : h + 1]
            value = v_ref[:, cols[h]].astype(f32)
            top = pred[h][:GROUP]
            target[h] = jnp.concatenate(
                [beta * (value - top[:, :DV]), -(beta * top[:, DV:])], axis=1
            )
        for h in hs:
            update[h] = nn(w_ref[0, :, h * GROUP : (h + 1) * GROUP], target[h]).astype(bf16)
        for h in hs:
            result = pred[h][GROUP:] + nn(scores[h], update[h])
            out_ref[:, cols[h]] = result[:, :DV]
            map_ref[:, cols[h]] = result[:, DV:].astype(bf16)
            up = grow[GROUP - 1 :, cols[h]]
            state[h] = entry[h] * up + tn(update[h], tail[h])

    @pl.when(step == pl.num_programs(0) - 1)
    def _():
        total_ref[...] = state[...]


def relay_kernel(n, forward, map_ref, add_ref, out_ref, arrive, depart, send_sem, recv_sem):
    me = lax.axis_index("seq")
    heads = out_ref.shape[0]
    if forward:
        has_source, has_target = me > 0, me < n - 1
        source, target = me - 1, me + 1
    else:
        has_source, has_target = me < n - 1, me > 0
        source, target = me + 1, me - 1

    barrier = pltpu.get_barrier_semaphore()

    @pl.when(has_source)
    def _():
        pl.semaphore_signal(barrier, inc=1, device_id={"seq": source}, device_id_type=MESH)

    @pl.when(has_target)
    def _():
        pl.semaphore_signal(barrier, inc=1, device_id={"seq": target}, device_id_type=MESH)

    @pl.when(jnp.logical_and(me > 0, me < n - 1))
    def _():
        pl.semaphore_wait(barrier, 2)

    if n > 1:
        @pl.when(jnp.logical_or(me == 0, me == n - 1))
        def _():
            pl.semaphore_wait(barrier, 1)

    def copy(h):
        return pltpu.make_async_remote_copy(
            src_ref=depart.at[h],
            dst_ref=arrive.at[h],
            send_sem=send_sem.at[h],
            recv_sem=recv_sem.at[h],
            device_id={"seq": target},
            device_id_type=MESH,
        )

    @pl.when(jnp.logical_not(has_source))
    def _():
        out_ref[...] = jnp.zeros_like(out_ref)

    for h in range(heads):
        @pl.when(has_source)
        def _():
            copy(h).wait_recv()
            out_ref[h] = arrive[h]

        @pl.when(has_target)
        def _():
            matrix = map_ref[h, DV:]
            high = matrix.astype(bf16)
            rest = matrix - high.astype(f32)
            now = out_ref[h]
            times = nn if forward else nt
            depart[h] = (add_ref[h, :DV] + (times(now, high) + times(now, rest))).astype(bf16)
            copy(h).start()

    @pl.when(has_target)
    def _():
        for h in range(heads):
            copy(h).wait_send()


def norm_kernel(in_ref, map_ref, s_ref, up_ref, gate_ref, gain_ref, go_ref, gg_ref, rest_ref):
    maps = map_ref[...]
    out = in_ref[...] + nt(maps, s_ref[0])
    scale = lax.rsqrt(jnp.mean(out * out, axis=-1, keepdims=True) + 1e-06)
    normal = out * scale
    sig = jax.nn.sigmoid(gate_ref[...].astype(f32))
    grad = up_ref[...] * gain_ref[...] * sig
    gg_ref[...] = (grad * normal * (1.0 - sig)).astype(bf16)
    inner = jnp.mean(grad * normal, axis=-1, keepdims=True)
    grad_out = (scale * (grad - normal * inner)).astype(bf16)
    go_ref[...] = grad_out
    rest_ref[0] = tn(grad_out, maps)


def grad_kernel(
    heads, together, resets, q_ref, k_ref, v_ref, g_ref, b_ref, w_ref, go_ref, enter_ref, s_ref,
    ds_ref, gq_ref, gk_ref, gv_ref, gd_ref, gb_ref, state,
):
    step = pl.program_id(0)
    chunk = pl.num_programs(0) - 1 - step

    @pl.when(step == 0)
    def _():
        state[...] = ds_ref[...].astype(f32)

    keep = jnp.where(chunk == resets[0], 0.0, 1.0)
    cumul = cumulative(g_ref[...])
    grow = jnp.exp(cumul)
    shrink = jnp.exp(-cumul)
    slopes = []
    for first in range(0, heads, together):
        hs = list(range(first, first + together))
        cols = {h: slice(h * DK, (h + 1) * DK) for h in hs}
        (entry, qd, kd, ki, kt, qh, kh, qs, ks, lows, err, update, scores, dscore, dup, dtar, dval,
         gout, past, dq, dk, di, dt, nxt, w) = ({} for _ in range(25))
        for h in hs:
            half = enter_ref[0, h]
            entry[h] = half[:DV].astype(f32) + nn(s_ref[h], half[DV:])
            qh[h], qs[h] = unit(q_ref[:, cols[h]].astype(f32))
            kh[h], ks[h] = unit(k_ref[:, cols[h]].astype(f32))
            up = grow[:, cols[h]]
            qd[h] = qh[h] * SCALE * up
            kd[h] = kh[h] * up
            ki[h] = kh[h] * shrink[:, cols[h]]
            kt[h] = ki[h] * up[GROUP - 1 :]
            gout[h] = go_ref[:, cols[h]]
            w[h] = w_ref[0, :, h * GROUP : (h + 1) * GROUP].astype(bf16)
            nxt[h] = state[h]
        for h in hs:
            lows[h] = entry[h].astype(bf16)
            scores[h] = lower_only(nt(qd[h], ki[h])).astype(bf16)
            err[h] = v_ref[:, cols[h]].astype(f32) - nt(kd[h], lows[h])
        for h in hs:
            update[h] = nn(w[h], b_ref[:, h : h + 1] * err[h]).astype(bf16)
            dup[h] = tn(scores[h], gout[h]) + nt(kt[h], nxt[h])
        for h in hs:
            dtar[h] = tn(w[h], dup[h])
            dscore[h] = lower_only(nt(gout[h], update[h])).astype(bf16)
        for h in hs:
            dval[h] = b_ref[:, h : h + 1] * dtar[h]
            gv_ref[:, cols[h]] = dval[h].astype(bf16)
            gb_ref[:, h : h + 1] = jnp.sum(dtar[h] * err[h], axis=-1, keepdims=True)
        for h in hs:
            both = jnp.concatenate([gout[h], -dval[h].astype(bf16)], axis=0)
            back = jnp.concatenate([qd[h].astype(bf16), kd[h].astype(bf16)], axis=0)
            up = grow[GROUP - 1 :, cols[h]]
            past[h] = nxt[h] * up
            state[h] = (past[h] + tn(both, back)) * keep
            through = nn(both, lows[h])
            dq[h] = through[:GROUP] + nn(dscore[h], ki[h])
            dk[h] = through[GROUP:]
            di[h] = tn(dscore[h], qd[h])
            dt[h] = nn(update[h], nxt[h])
        for h in hs:
            up = grow[:, cols[h]]
            tailed = dt[h] * kt[h]
            last = jnp.sum(past[h] * entry[h], axis=0, keepdims=True) + jnp.sum(
                tailed, axis=0, keepdims=True
            )
            slope = dq[h] * qd[h] + dk[h] * kd[h] - di[h] * ki[h] - tailed
            slopes.append((slope, last))
            gq = dq[h] * up
            gk = dk[h] * up + (di[h] + dt[h] * up[GROUP - 1 :]) * shrink[:, cols[h]]
            gq = (gq - qh[h] * jnp.sum(gq * qh[h], axis=-1, keepdims=True)) * (qs[h] * SCALE)
            gk = (gk - kh[h] * jnp.sum(gk * kh[h], axis=-1, keepdims=True)) * ks[h]
            gq_ref[:, cols[h]] = gq.astype(bf16)
            gk_ref[:, cols[h]] = gk.astype(bf16)
    slope = jnp.concatenate([a for a, _ in slopes], axis=1)
    last = jnp.concatenate([b for _, b in slopes], axis=1)
    gd_ref[...] = nn(triangle(True, 2), split_rows(slope, 2)) + last


def params(**more):
    return pltpu.CompilerParams(vmem_limit_bytes=VMEM_LIMIT, **more)


def relay(n, forward, maps, add):
    heads = maps.shape[0]
    whole = pl.BlockSpec(memory_space=pltpu.VMEM)
    return pl.pallas_call(
        functools.partial(relay_kernel, n, forward),
        out_shape=jax.ShapeDtypeStruct((heads, DV, DK), bf16),
        in_specs=[whole, whole],
        out_specs=whole,
        scratch_shapes=[
            pltpu.VMEM((heads, DV, DK), bf16),
            pltpu.VMEM((heads, DV, DK), bf16),
            pltpu.SemaphoreType.DMA((heads,)),
            pltpu.SemaphoreType.DMA((heads,)),
        ],
        compiler_params=params(collective_id=0 if forward else 1, has_side_effects=True),
        name="relay_forward" if forward else "relay_back",
    )(maps, add)


def per_device(
    n, queries, keys, values, decay, beta, wy_inverse, out_gate, norm_gain, out_proj, grad_out,
    resets,
):
    tokens, width = queries.shape
    heads = beta.shape[0]
    count = tokens // GROUP
    together = 4 if heads % 4 == 0 else 1
    gathered = lax.all_gather(grad_out, "head", axis=1, tiled=True)
    beta_rows = beta.T

    def rows(step):
        return (step, 0)

    def rows_back(step):
        return (count - 1 - step, 0)

    scalar = pl.BlockSpec(memory_space=pltpu.SMEM)
    tile = pl.BlockSpec((GROUP, width), rows)
    out_local, maps, enter, total = pl.pallas_call(
        functools.partial(local_kernel, heads, together),
        grid=(count,),
        in_specs=[
            scalar, tile, tile, tile, tile,
            pl.BlockSpec((GROUP, heads), rows),
            pl.BlockSpec((1, GROUP, heads * GROUP), lambda i: (i, 0, 0)),
        ],
        out_specs=[
            tile, tile,
            pl.BlockSpec((1, heads, DV + DK, DK), lambda i: (i, 0, 0, 0)),
            pl.BlockSpec((heads, DV + DK, DK), lambda i: (0, 0, 0)),
        ],
        out_shape=[
            jax.ShapeDtypeStruct((tokens, width), f32),
            jax.ShapeDtypeStruct((tokens, width), bf16),
            jax.ShapeDtypeStruct((count, heads, DV + DK, DK), bf16),
            jax.ShapeDtypeStruct((heads, DV + DK, DK), f32),
        ],
        scratch_shapes=[pltpu.VMEM((heads, DV + DK, DK), f32)],
        compiler_params=params(),
        name="local",
    )(resets, queries, keys, values, decay, beta_rows, wy_inverse)

    state_in = relay(n, True, total, total)

    upstream = lax.dot_general(
        gathered, out_proj, (((1,), (1,)), ((), ())), preferred_element_type=f32
    )
    column = pl.BlockSpec((tokens, DV), lambda h: (0, h))
    square = pl.BlockSpec((1, DV, DK), lambda h: (h, 0, 0))
    grad_raw, grad_gate, rest = pl.pallas_call(
        norm_kernel,
        grid=(heads,),
        in_specs=[
            column, column, square, column, column,
            pl.BlockSpec((1, DV), lambda h: (0, 0)),
        ],
        out_specs=[column, column, square],
        out_shape=[
            jax.ShapeDtypeStruct((tokens, width), bf16),
            jax.ShapeDtypeStruct((tokens, width), bf16),
            jax.ShapeDtypeStruct((heads, DV, DK), f32),
        ],
        compiler_params=params(),
        name="norm",
    )(out_local, maps, state_in, upstream, out_gate, norm_gain.reshape(1, DV))

    state_grad = relay(n, False, total, rest)

    tile = pl.BlockSpec((GROUP, width), rows_back)
    whole = pl.BlockSpec((heads, DV, DK), lambda i: (0, 0, 0))
    thin = pl.BlockSpec((GROUP, heads), rows_back)
    grad_query, grad_key, grad_value, grad_decay, grad_beta = pl.pallas_call(
        functools.partial(grad_kernel, heads, together),
        grid=(count,),
        in_specs=[
            scalar, tile, tile, tile, tile, thin,
            pl.BlockSpec((1, GROUP, heads * GROUP), lambda i: (count - 1 - i, 0, 0)),
            tile,
            pl.BlockSpec((1, heads, DV + DK, DK), lambda i: (count - 1 - i, 0, 0, 0)),
            whole, whole,
        ],
        out_specs=[tile, tile, tile, tile, thin],
        out_shape=[
            jax.ShapeDtypeStruct((tokens, width), bf16),
            jax.ShapeDtypeStruct((tokens, width), bf16),
            jax.ShapeDtypeStruct((tokens, width), bf16),
            jax.ShapeDtypeStruct((tokens, width), f32),
            jax.ShapeDtypeStruct((tokens, heads), f32),
        ],
        scratch_shapes=[pltpu.VMEM((heads, DV, DK), f32)],
        compiler_params=params(),
        name="grad",
    )(
        resets, queries, keys, values, decay, beta_rows, wy_inverse, grad_raw, enter, state_in,
        state_grad,
    )
    return (grad_query, grad_key, grad_value, grad_decay, grad_beta.T, grad_gate)


def solution(mesh):
    tokens_heads = P("seq", "head")
    return jax.shard_map(
        functools.partial(per_device, mesh.shape["seq"]),
        mesh=mesh,
        in_specs=(
            tokens_heads, tokens_heads, tokens_heads, tokens_heads,
            P("head", "seq"), P("seq", None, "head"), tokens_heads, P(), P("head", None),
            tokens_heads, P("seq"),
        ),
        out_specs=(
            tokens_heads, tokens_heads, tokens_heads, tokens_heads, P("head", "seq"), tokens_heads,
        ),
        check_vma=False,
    )
```

time: 1920 us -> 163 us (0.08); the launches traced: 1890 us -> 162 us
  matrix products: 695 us -> 9.92 us
  local copies, waits for them, and re-layouts: 554 us -> 6.03 us
  other arithmetic: 463 us -> 0 us
  Pallas kernels: 0 us -> 128 us
  waiting for transfers between devices: 105 us -> 3.84 us
  starting transfers between devices: 51.3 us -> 0.04 us
    dot_general x593 -> x1, matrix products: 695 us -> 9.92 us  [per_device(): lax.dot_general(gathered, out_proj, (((1,), (1,)), ((), ())), preferred_e...]
    another operation x128 -> x0, other arithmetic: 284 us -> none  [the longest x96 267 us: group_step(): cumul = jnp.cumsum(gate_rows, axis=1)]
    squeeze x304 -> x0, local copies, waits for them, and re-layouts: 242 us -> none  [the longest x256 242 us: core(): final, outputs = lax.scan(jax.checkpoint(group_step), state, blocks)]
    pallas_call x0 -> x5, Pallas kernels: none -> 128 us  [the longest x2 52.6 us: relay(): pl.pallas_call(functools.partial(relay_kernel, n, forward), out_shape=jax...]
    dynamic_slice x128 -> x0, local copies, waits for them, and re-layouts: 113 us -> none  [core(): final, outputs = lax.scan(jax.checkpoint(group_step), state, blocks)]
    ppermute x16 -> x0, waiting for transfers between devices: 104 us -> none  [from_behind(): return lax.ppermute(x, axis, pairs)]
    dynamic_update_slice x80 -> x0, local copies, waits for them, and re-layouts: 68.4 us -> none  [core(): final, outputs = lax.scan(jax.checkpoint(group_step), state, blocks)]
    convert_element_type x54 -> x0, other arithmetic: 64 us -> none  [the longest x16 19.1 us: low_product(): right.astype(jnp.bfloat16)]
  transfers between devices with their start and end apart: 17 -> 1, of which waited for: 16 -> 1; matrix products, arithmetic and copies ran while one was open for 27% -> 1% of each run, Pallas kernels for 0% -> 21%
where the time goes in v1:
time: 163 us; the launch traced here: 162 us
  Pallas kernels  128 us (79%)
  between operations  14.7 us (9%)
  matrix products  9.92 us (6%)
  local copies, waits for them, and re-layouts  6.03 us (4%)
  waiting for transfers between devices  3.84 us (2%)
    pallas_call x2, Pallas kernels, relay(): pl.pallas_call(functools.partial(relay_kernel, n, forward), out_shape=jax...  52.6 us
    pallas_call x1, Pallas kernels, per_device(): pl.pallas_call(functools.partial(grad_kernel, heads, together), grid=(cou...  39 us
    pallas_call x1, Pallas kernels, per_device(): pl.pallas_call(functools.partial(local_kernel, heads, together), grid=(co...  25.3 us
    pallas_call x1, Pallas kernels, per_device(): pl.pallas_call(norm_kernel, grid=(heads,), in_specs=[column, column, squa...  10.8 us
    dot_general x1, matrix products, per_device(): lax.dot_general(gathered, out_proj, (((1,), (1,)), ((), ())), preferred_e...  9.92 us
    unnamed x16, local copies, waits for them, and re-layouts  6.03 us
  transfers between devices with their start and end apart: 1, of which 1 were waited for; matrix products, arithmetic and copies ran while one was open for 1% of the time, Pallas kernels for 21%

profile of v1, /device:TPU:0, one launch (start us, length us, event | category | flops | bytes accessed | tf_op | source)
XLA Modules:
  0.0 162.3 jit_solution(15268904868610692139)
XLA Ops:
  7.2 0.0 all-gather.2.cloned.1.call-start
  7.2 0.7 all-gather.2.cloned.1.call-update
  8.5 1.0 copy.17
  9.5 0.0 copy-start
  9.5 1.6 copy-done
  11.1 25.3 %local.1 = (f32[1024,1024]{1,0:T(8,128)}, bf16[1024,1024]{1,0:T(8,128)(2,1)S(1)}, bf16[16,8,256,128]{3,2,1,0:T(8,128)(2,1)}, f32[8,256,128]{2,1,0:T(8,128)S(1)}) custom-call(s32[1]{0:T(128)S(6)} %copy.19.resets, bf16[1024,1024]{1,0:T(8,128)(2,1)S(1)} %copy-done, bf16[1024,1024]{1,0:T(8,128)(2,1)} %k_ref.3, bf16[1024,1024]{1,0:T(8,128)(2,1)} %v_ref.3, ...), custom_call_target="tpu_custom_call" | custom-call | tf_op jit(solution)/shard_map/local/pallas_call | solution.py:327
  36.4 0.0 copy-start.3
  36.4 1.3 copy-done.3
  37.7 8.9 %relay_forward.1.s_ref = bf16[8,128,128]{2,1,0:T(8,128)(2,1)S(1)} custom-call(f32[8,256,128]{2,1,0:T(8,128)S(1)} %get-tuple-element.20.map_ref.add_ref, f32[8,256,128]{2,1,0:T(8,128)S(1)} %get-tuple-element.20.map_ref.add_ref), custom_call_target="tpu_custom_call" | custom-call | tf_op jit(solution)/shard_map/relay_forward/pallas_call | solution.py:292
  46.6 0.0 copy-start.6
  46.6 3.2 %all-gather.2.cloned.1.call-done = bf16[1024,2304]{0,1:T(8,128)(2,1)} async-done(((bf16[1024,576]{0,1:T(8,128)(2,1)}), bf16[1024,2304]{0,1:T(8,128)(2,1)}) %all-gather.2.cloned.1.call-update) | async-done | bytes 4718608 | tf_op jit(solution)/shard_map/all_gather | solution.py:316
  49.8 0.0 copy-start.4
  49.8 9.9 %fusion.up_ref = f32[1024,1024]{1,0:T(8,128)} fusion(bf16[1024,2304]{0,1:T(8,128)(2,1)} %all-gather.2.cloned.1.call-done, bf16[1024,2304]{1,0:T(8,128)(2,1)} %param.19), kind=kOutput, calls=%fused_computation | convolution fusion | flops 4831838208 | bytes 13631488 | tf_op jit(solution)/shard_map/dot_general | solution.py:353
  59.7 0.0 copy-done.6
  59.7 0.0 copy-done.4
  59.7 0.0 copy-start.1
  59.7 0.0 copy-start.2
  59.8 10.8 %norm.1 = (bf16[1024,1024]{1,0:T(8,128)(2,1)S(1)}, bf16[1024,1024]{1,0:T(8,128)(2,1)}, f32[8,128,128]{2,1,0:T(8,128)S(1)}) custom-call(f32[1024,1024]{1,0:T(8,128)} %get-tuple-element.18.in_ref, bf16[1024,1024]{1,0:T(8,128)(2,1)S(1)} %copy-done.4, bf16[8,128,128]{2,1,0:T(8,128)(2,1)S(1)} %relay_forward.1.s_ref, f32[1024,1024]{1,0:T(8,128)} %fusion.up_ref, ...), custom_call_target="tpu_custom_call" | custom-call | tf_op jit(solution)/shard_map/norm/pallas_call | solution.py:358
  70.6 1.4 copy-done.5
  72.0 43.7 %relay_back.1.ds_ref = bf16[8,128,128]{2,1,0:T(8,128)(2,1)S(1)} custom-call(f32[8,256,128]{2,1,0:T(8,128)S(1)} %get-tuple-element.20.map_ref.add_ref, f32[8,128,128]{2,1,0:T(8,128)S(1)} %get-tuple-element.23.add_ref), custom_call_target="tpu_custom_call" | custom-call | tf_op jit(solution)/shard_map/relay_back/pallas_call | solution.py:292
  115.7 0.0 copy-done.1
  115.7 0.0 copy-done.2
  115.7 39.0 %grad.1 = (bf16[1024,1024]{1,0:T(8,128)(2,1)}, bf16[1024,1024]{1,0:T(8,128)(2,1)}, bf16[1024,1024]{1,0:T(8,128)(2,1)}, f32[1024,1024]{1,0:T(8,128)}, f32[1024,8]{1,0:T(8,128)S(1)}) custom-call(s32[1]{0:T(128)S(6)} %copy.19.resets, bf16[1024,1024]{1,0:T(8,128)(2,1)S(1)} %copy-done.1, bf16[1024,1024]{1,0:T(8,128)(2,1)S(1)} %copy-done.2, ...), custom_call_target="tpu_custom_call" | custom-call | tf_op jit(solution)/shard_map/grad/pallas_call | solution.py:380
  154.7 0.8 copy.18
  (1 shorter events, 0.0 us)
Async XLA Ops:
  7.2 42.6 %all-gather.2.cloned.1.call-start = ((), (), s32[]{:S(2)}) async-start(), calls=%async_computation | async-start | bytes 5898240 | tf_op jit(solution)/shard_map/all_gather | solution.py:316
  9.5 1.6 copy-start
  36.4 1.3 copy-start.3
  46.6 13.1 %copy-start.6 = (f32[128]{0:T(128)S(1)}, f32[128]{0:T(128)}, u32[]{:S(2)}) copy-start(f32[128]{0:T(128)} %param.18) | copy-start | bytes 1540
  49.8 9.9 %copy-start.4 = (bf16[1024,1024]{1,0:T(8,128)(2,1)S(1)}, bf16[1024,1024]{1,0:T(8,128)(2,1)}, u32[]{:S(2)}) copy-start(bf16[1024,1024]{1,0:T(8,128)(2,1)} %copy-done.3) | copy-start | bytes 6291460
  59.7 56.0 %copy-start.1 = (bf16[1024,1024]{1,0:T(8,128)(2,1)S(1)}, bf16[1024,1024]{1,0:T(8,128)(2,1)}, u32[]{:S(2)}) copy-start(bf16[1024,1024]{1,0:T(8,128)(2,1)} %q_ref.3) | copy-start | bytes 6291460
  59.7 56.0 %copy-start.2 = (bf16[1024,1024]{1,0:T(8,128)(2,1)S(1)}, bf16[1024,1024]{1,0:T(8,128)(2,1)}, u32[]{:S(2)}) copy-start(bf16[1024,1024]{1,0:T(8,128)(2,1)} %k_ref.3) | copy-start | bytes 6291460
  70.6 1.4 copy-start.5
Sparse Core Ops, SparseCore 0:
  9.6 40.2 all-gather.1

commit v2 on v1

--- a/solution.py
+++ b/solution.py
@@ -196,7 +196,7 @@
     scale = lax.rsqrt(jnp.mean(out * out, axis=-1, keepdims=True) + 1e-06)
     normal = out * scale
     sig = jax.nn.sigmoid(gate_ref[...].astype(f32))
-    grad = up_ref[...] * gain_ref[...] * sig
+    grad = up_ref[...].astype(f32) * gain_ref[...] * sig
     gg_ref[...] = (grad * normal * (1.0 - sig)).astype(bf16)
     inner = jnp.mean(grad * normal, axis=-1, keepdims=True)
     grad_out = (scale * (grad - normal * inner)).astype(bf16)
@@ -204,9 +204,61 @@
     rest_ref[0] = tn(grad_out, maps)
 
 
+def prepare_kernel(
+    heads, together, span, q_ref, k_ref, v_ref, g_ref, b_ref, w_ref, go_ref, enter_ref, s_ref,
+    *refs,
+):
+    gq_ref, qd_ref, low_ref, up_ref, err_ref, dup_ref, part_ref, di_ref = refs[-8:]
+    step = pl.program_id(0)
+
+    @pl.when(jnp.logical_and(step >= span[0], step < span[1]))
+    def _():
+        cumul = cumulative(g_ref[...])
+        grow = jnp.exp(cumul)
+        shrink = jnp.exp(-cumul)
+        for first in range(0, heads, together):
+            hs = list(range(first, first + together))
+            cols = {h: slice(h * DK, (h + 1) * DK) for h in hs}
+            low, qd, kd, ki, qh, qs, err, update, scores, gout, dscore, dq, di = (
+                {} for _ in range(13)
+            )
+            for h in hs:
+                half = enter_ref[0, h]
+                low[h] = (half[:DV].astype(f32) + nn(s_ref[h], half[DV:])).astype(bf16)
+                low_ref[0, h] = low[h]
+                qh[h], qs[h] = unit(q_ref[:, cols[h]].astype(f32))
+                kh = unit(k_ref[:, cols[h]].astype(f32))[0]
+                up = grow[:, cols[h]]
+                qd[h] = qh[h] * SCALE * up
+                kd[h] = (kh * up).astype(bf16)
+                ki[h] = kh * shrink[:, cols[h]]
+                qd_ref[:, cols[h]] = qd[h].astype(bf16)
+                gout[h] = go_ref[:, cols[h]]
+            for h in hs:
+                scores[h] = lower_only(nt(qd[h], ki[h])).astype(bf16)
+                err[h] = v_ref[:, cols[h]].astype(f32) - nt(kd[h], low[h])
+                err_ref[:, cols[h]] = err[h].astype(bf16)
+            for h in hs:
+                w = w_ref[0, :, h * GROUP : (h + 1) * GROUP]
+                update[h] = nn(w, b_ref[:, h : h + 1] * err[h]).astype(bf16)
+                up_ref[:, cols[h]] = update[h]
+                dup_ref[:, cols[h]] = tn(scores[h], gout[h]).astype(bf16)
+            for h in hs:
+                dscore[h] = lower_only(nt(gout[h], update[h])).astype(bf16)
+            for h in hs:
+                dq[h] = nn(gout[h], low[h]) + nn(dscore[h], ki[h])
+                di[h] = tn(dscore[h], qd[h])
+            for h in hs:
+                part_ref[:, cols[h]] = dq[h] * qd[h] - di[h] * ki[h]
+                di_ref[:, cols[h]] = (di[h] * shrink[:, cols[h]]).astype(bf16)
+                gq = dq[h] * grow[:, cols[h]]
+                gq = (gq - qh[h] * jnp.sum(gq * qh[h], axis=-1, keepdims=True)) * (qs[h] * SCALE)
+                gq_ref[:, cols[h]] = gq.astype(bf16)
+
+
 def grad_kernel(
-    heads, together, resets, q_ref, k_ref, v_ref, g_ref, b_ref, w_ref, go_ref, enter_ref, s_ref,
-    ds_ref, gq_ref, gk_ref, gv_ref, gd_ref, gb_ref, state,
+    heads, together, resets, k_ref, g_ref, b_ref, w_ref, go_ref, qd_ref, low_ref, up_ref, err_ref,
+    dup_ref, part_ref, di_ref, ds_ref, gk_ref, gv_ref, gd_ref, gb_ref, state,
 ):
     step = pl.program_id(0)
     chunk = pl.num_programs(0) - 1 - step
@@ -223,59 +275,40 @@
     for first in range(0, heads, together):
         hs = list(range(first, first + together))
         cols = {h: slice(h * DK, (h + 1) * DK) for h in hs}
-        (entry, qd, kd, ki, kt, qh, kh, qs, ks, lows, err, update, scores, dscore, dup, dtar, dval,
-         gout, past, dq, dk, di, dt, nxt, w) = ({} for _ in range(25))
-        for h in hs:
-            half = enter_ref[0, h]
-            entry[h] = half[:DV].astype(f32) + nn(s_ref[h], half[DV:])
-            qh[h], qs[h] = unit(q_ref[:, cols[h]].astype(f32))
+        kd, kt, kh, ks, dup, dtar, dval, past, dk, dt, nxt = ({} for _ in range(11))
+        for h in hs:
             kh[h], ks[h] = unit(k_ref[:, cols[h]].astype(f32))
             up = grow[:, cols[h]]
-            qd[h] = qh[h] * SCALE * up
             kd[h] = kh[h] * up
-            ki[h] = kh[h] * shrink[:, cols[h]]
-            kt[h] = ki[h] * up[GROUP - 1 :]
-            gout[h] = go_ref[:, cols[h]]
-            w[h] = w_ref[0, :, h * GROUP : (h + 1) * GROUP].astype(bf16)
+            kt[h] = kh[h] * shrink[:, cols[h]] * up[GROUP - 1 :]
             nxt[h] = state[h]
         for h in hs:
-            lows[h] = entry[h].astype(bf16)
-            scores[h] = lower_only(nt(qd[h], ki[h])).astype(bf16)
-            err[h] = v_ref[:, cols[h]].astype(f32) - nt(kd[h], lows[h])
-        for h in hs:
-            update[h] = nn(w[h], b_ref[:, h : h + 1] * err[h]).astype(bf16)
-            dup[h] = tn(scores[h], gout[h]) + nt(kt[h], nxt[h])
-        for h in hs:
-            dtar[h] = tn(w[h], dup[h])
-            dscore[h] = lower_only(nt(gout[h], update[h])).astype(bf16)
-        for h in hs:
-            dval[h] = b_ref[:, h : h + 1] * dtar[h]
-            gv_ref[:, cols[h]] = dval[h].astype(bf16)
-            gb_ref[:, h : h + 1] = jnp.sum(dtar[h] * err[h], axis=-1, keepdims=True)
-        for h in hs:
-            both = jnp.concatenate([gout[h], -dval[h].astype(bf16)], axis=0)
-            back = jnp.concatenate([qd[h].astype(bf16), kd[h].astype(bf16)], axis=0)
-            up = grow[GROUP - 1 :, cols[h]]
-            past[h] = nxt[h] * up
+            dup[h] = dup_ref[:, cols[h]].astype(f32) + nt(kt[h], nxt[h])
+        for h in hs:
+            dtar[h] = tn(w_ref[0, :, h * GROUP : (h + 1) * GROUP], dup[h])
+            dt[h] = nn(up_ref[:, cols[h]], nxt[h])
+        for h in hs:
+            dval[h] = (b_ref[:, h : h + 1] * dtar[h]).astype(bf16)
+            gv_ref[:, cols[h]] = dval[h]
+            gb_ref[:, h : h + 1] = jnp.sum(
+                dtar[h] * err_ref[:, cols[h]].astype(f32), axis=-1, keepdims=True
+            )
+        for h in hs:
+            both = jnp.concatenate([go_ref[:, cols[h]], -dval[h]], axis=0)
+            back = jnp.concatenate([qd_ref[:, cols[h]], kd[h].astype(bf16)], axis=0)
+            past[h] = nxt[h] * grow[GROUP - 1 :, cols[h]]
             state[h] = (past[h] + tn(both, back)) * keep
-            through = nn(both, lows[h])
-            dq[h] = through[:GROUP] + nn(dscore[h], ki[h])
-            dk[h] = through[GROUP:]
-            di[h] = tn(dscore[h], qd[h])
-            dt[h] = nn(update[h], nxt[h])
+            dk[h] = -nn(dval[h], low_ref[0, h])
         for h in hs:
             up = grow[:, cols[h]]
             tailed = dt[h] * kt[h]
-            last = jnp.sum(past[h] * entry[h], axis=0, keepdims=True) + jnp.sum(
+            last = jnp.sum(past[h] * low_ref[0, h].astype(f32), axis=0, keepdims=True) + jnp.sum(
                 tailed, axis=0, keepdims=True
             )
-            slope = dq[h] * qd[h] + dk[h] * kd[h] - di[h] * ki[h] - tailed
-            slopes.append((slope, last))
-            gq = dq[h] * up
-            gk = dk[h] * up + (di[h] + dt[h] * up[GROUP - 1 :]) * shrink[:, cols[h]]
-            gq = (gq - qh[h] * jnp.sum(gq * qh[h], axis=-1, keepdims=True)) * (qs[h] * SCALE)
+            slopes.append((part_ref[:, cols[h]] + dk[h] * kd[h] - tailed, last))
+            gk = dk[h] * up + dt[h] * (up[GROUP - 1 :] * shrink[:, cols[h]])
+            gk = gk + di_ref[:, cols[h]].astype(f32)
             gk = (gk - kh[h] * jnp.sum(gk * kh[h], axis=-1, keepdims=True)) * ks[h]
-            gq_ref[:, cols[h]] = gq.astype(bf16)
             gk_ref[:, cols[h]] = gk.astype(bf16)
     slope = jnp.concatenate([a for a, _ in slopes], axis=1)
     last = jnp.concatenate([b for _, b in slopes], axis=1)
@@ -325,7 +358,7 @@
     scalar = pl.BlockSpec(memory_space=pltpu.SMEM)
     tile = pl.BlockSpec((GROUP, width), rows)
     out_local, maps, enter, total = pl.pallas_call(
-        functools.partial(local_kernel, heads, together),
+        functools.partial(local_kernel, heads, heads),
         grid=(count,),
         in_specs=[
             scalar, tile, tile, tile, tile,
@@ -351,7 +384,7 @@
     state_in = relay(n, True, total, total)
 
     upstream = lax.dot_general(
-        gathered, out_proj, (((1,), (1,)), ((), ())), preferred_element_type=f32
+        gathered, out_proj, (((1,), (1,)), ((), ())), preferred_element_type=bf16
     )
     column = pl.BlockSpec((tokens, DV), lambda h: (0, h))
     square = pl.BlockSpec((1, DV, DK), lambda h: (h, 0, 0))
@@ -372,24 +405,74 @@
         name="norm",
     )(out_local, maps, state_in, upstream, out_gate, norm_gain.reshape(1, DV))
 
+    whole = pl.BlockSpec((heads, DV, DK), lambda i, *_: (0, 0, 0))
+
+    def prepare(start, stop, earlier):
+        def chunk(i, span):
+            return jnp.minimum(jnp.maximum(i, span[0]), span[1] - 1)
+
+        def at(i, span):
+            return (chunk(i, span), 0)
+
+        block = pl.BlockSpec((GROUP, width), at)
+        low = pl.BlockSpec((1, heads, DV, DK), lambda i, span: (chunk(i, span), 0, 0, 0))
+        any_place = pl.BlockSpec(memory_space=pl.ANY)
+        wide = jax.ShapeDtypeStruct((tokens, width), bf16)
+        out_shape = [
+            wide, wide, jax.ShapeDtypeStruct((count, heads, DV, DK), bf16), wide, wide, wide,
+            jax.ShapeDtypeStruct((tokens, width), f32), wide,
+        ]
+        inputs = (
+            queries, keys, values, decay, beta_rows, wy_inverse, grad_raw, enter, state_in,
+        )
+        return pl.pallas_call(
+            functools.partial(prepare_kernel, heads, together),
+            grid_spec=pltpu.PrefetchScalarGridSpec(
+                num_scalar_prefetch=1,
+                grid=(count,),
+                in_specs=[
+                    block, block, block, block,
+                    pl.BlockSpec((GROUP, heads), at),
+                    pl.BlockSpec((1, GROUP, heads * GROUP), lambda i, span: (chunk(i, span), 0, 0)),
+                    block,
+                    pl.BlockSpec(
+                        (1, heads, DV + DK, DK), lambda i, span: (chunk(i, span), 0, 0, 0)
+                    ),
+                    whole,
+                ]
+                + [any_place] * len(earlier),
+                out_specs=[block, block, low, block, block, block, block, block],
+            ),
+            out_shape=out_shape,
+            input_output_aliases={1 + len(inputs) + i: i for i in range(len(earlier))},
+            compiler_params=params(),
+            name="prepare",
+        )(jnp.stack([start, stop]), *inputs, *earlier)
+
+    away = n - 1 - lax.axis_index("seq")
+    ahead = jnp.minimum(jnp.maximum(2 * away - 1, 1), count - 1).astype(jnp.int32)
+    begun = prepare(jnp.int32(0), ahead, ())
+    begun, rest = lax.optimization_barrier((begun, rest))
     state_grad = relay(n, False, total, rest)
+    begun, state_grad = lax.optimization_barrier((begun, state_grad))
+    grad_query, qd, low, update, err, dup, part, di = prepare(
+        ahead, jnp.int32(count), tuple(begun)
+    )
 
     tile = pl.BlockSpec((GROUP, width), rows_back)
-    whole = pl.BlockSpec((heads, DV, DK), lambda i: (0, 0, 0))
     thin = pl.BlockSpec((GROUP, heads), rows_back)
-    grad_query, grad_key, grad_value, grad_decay, grad_beta = pl.pallas_call(
+    grad_key, grad_value, grad_decay, grad_beta = pl.pallas_call(
         functools.partial(grad_kernel, heads, together),
         grid=(count,),
         in_specs=[
-            scalar, tile, tile, tile, tile, thin,
+            scalar, tile, tile, thin,
             pl.BlockSpec((1, GROUP, heads * GROUP), lambda i: (count - 1 - i, 0, 0)),
-            tile,
-            pl.BlockSpec((1, heads, DV + DK, DK), lambda i: (count - 1 - i, 0, 0, 0)),
-            whole, whole,
-        ],
-        out_specs=[tile, tile, tile, tile, thin],
+            tile, tile,
+            pl.BlockSpec((1, heads, DV, DK), lambda i: (count - 1 - i, 0, 0, 0)),
+            tile, tile, tile, tile, tile, whole,
+        ],
+        out_specs=[tile, tile, tile, thin],
         out_shape=[
-            jax.ShapeDtypeStruct((tokens, width), bf16),
             jax.ShapeDtypeStruct((tokens, width), bf16),
             jax.ShapeDtypeStruct((tokens, width), bf16),
             jax.ShapeDtypeStruct((tokens, width), f32),
@@ -399,7 +482,7 @@
         compiler_params=params(),
         name="grad",
     )(
-        resets, queries, keys, values, decay, beta_rows, wy_inverse, grad_raw, enter, state_in,
+        resets, keys, decay, beta_rows, wy_inverse, grad_raw, qd, low, update, err, dup, part, di,
         state_grad,
     )
     return (grad_query, grad_key, grad_value, grad_decay, grad_beta.T, grad_gate)

time: 163 us -> 166 us (1.018)
  Pallas kernels: 128 us -> 124 us
  waiting for transfers between devices: 3.84 us -> 6.92 us
  local copies, waits for them, and re-layouts: 6.03 us -> 8.67 us
    pallas_call x1 -> x3, Pallas kernels: 25.3 us -> 60.7 us  [the longest x2 38.6 us: prepare(): pl.pallas_call(functools.partial(prepare_kernel, heads, together), grid_s...]
    pallas_call x2, Pallas kernels: 52.6 us -> 29 us  [relay(): pl.pallas_call(functools.partial(relay_kernel, n, forward), out_shape=jax...]
    pallas_call x1, Pallas kernels: 39 us -> 24.3 us  [per_device(): pl.pallas_call(functools.partial(grad_kernel, heads, together), grid=(cou...]
    all_gather x1, waiting for transfers between devices: 3.16 us -> 6.24 us  [per_device(): gathered = lax.all_gather(grad_out, 'head', axis=1, tiled=True)]
    unnamed x16 -> x20, local copies, waits for them, and re-layouts: 6.03 us -> 8.67 us
  transfers between devices with their start and end apart: 1 -> 1, of which waited for: 1 -> 1; matrix products, arithmetic and copies ran while one was open for 1% -> 1% of each run, Pallas kernels for 21% -> 19%
where the time goes in v2:
time: 166 us; the launch traced here: 164 us
  Pallas kernels  124 us (75%)
  between operations  14.7 us (9%)
  matrix products  9.49 us (6%)
  local copies, waits for them, and re-layouts  8.67 us (5%)
  waiting for transfers between devices  6.92 us (4%)
    pallas_call x2, Pallas kernels, prepare(): pl.pallas_call(functools.partial(prepare_kernel, heads, together), grid_s...  38.6 us
    pallas_call x2, Pallas kernels, relay(): pl.pallas_call(functools.partial(relay_kernel, n, forward), out_shape=jax...  29 us
    pallas_call x1, Pallas kernels, per_device(): pl.pallas_call(functools.partial(grad_kernel, heads, together), grid=(cou...  24.3 us
    pallas_call x1, Pallas kernels, per_device(): pl.pallas_call(functools.partial(local_kernel, heads, heads), grid=(count...  22.1 us
    pallas_call x1, Pallas kernels, per_device(): pl.pallas_call(norm_kernel, grid=(heads,), in_specs=[column, column, squa...  10.4 us
    dot_general x1, matrix products, per_device(): lax.dot_general(gathered, out_proj, (((1,), (1,)), ((), ())), preferred_e...  9.49 us
    unnamed x20, local copies, waits for them, and re-layouts  8.67 us
    all_gather x1, waiting for transfers between devices, per_device(): gathered = lax.all_gather(grad_out, 'head', axis=1, tiled=True)  6.24 us
  transfers between devices with their start and end apart: 1, of which 1 were waited for; matrix products, arithmetic and copies ran while one was open for 1% of the time, Pallas kernels for 19%

profile of v2, /device:TPU:0, one launch (start us, length us, event | category | flops | bytes accessed | tf_op | source)
XLA Modules:
  0.0 164.4 jit_solution(12896558332864910398)
XLA Ops:
  7.2 0.0 all-gather.2.cloned.1.call-start
  7.2 0.7 all-gather.2.cloned.1.call-update
  8.5 1.0 copy.25
  9.5 0.0 copy-start.2
  9.5 1.6 copy-done.2
  11.1 22.1 %local.1 = (f32[1024,1024]{1,0:T(8,128)}, bf16[1024,1024]{1,0:T(8,128)(2,1)S(1)}, bf16[16,8,256,128]{3,2,1,0:T(8,128)(2,1)}, f32[8,256,128]{2,1,0:T(8,128)S(1)}) custom-call(s32[1]{0:T(128)S(6)} %copy.35.resets, bf16[1024,1024]{1,0:T(8,128)(2,1)S(1)} %copy-done.2, bf16[1024,1024]{1,0:T(8,128)(2,1)} %k_ref.7, bf16[1024,1024]{1,0:T(8,128)(2,1)} %v_ref.5, ...), custom_call_target="tpu_custom_call" | custom-call | tf_op jit(solution)/shard_map/local/pallas_call | solution.py:360
  33.3 1.3 copy-done.6
  34.6 8.8 %relay_forward.1.s_ref = bf16[8,128,128]{2,1,0:T(8,128)(2,1)S(1)} custom-call(f32[8,256,128]{2,1,0:T(8,128)S(1)} %get-tuple-element.53.map_ref.add_ref, f32[8,256,128]{2,1,0:T(8,128)S(1)} %get-tuple-element.53.map_ref.add_ref), custom_call_target="tpu_custom_call" | custom-call | tf_op jit(solution)/shard_map/relay_forward/pallas_call | solution.py:325
  43.4 0.1 pad_add_fusion
  43.5 6.2 %all-gather.2.cloned.1.call-done = bf16[1024,2304]{0,1:T(8,128)(2,1)} async-done(((bf16[1024,576]{0,1:T(8,128)(2,1)}), bf16[1024,2304]{0,1:T(8,128)(2,1)}) %all-gather.2.cloned.1.call-update) | async-done | bytes 4718608 | tf_op jit(solution)/shard_map/all_gather | solution.py:349
  49.8 9.5 %fusion.up_ref = bf16[1024,1024]{1,0:T(8,128)(2,1)} fusion(bf16[1024,2304]{0,1:T(8,128)(2,1)} %all-gather.2.cloned.1.call-done, bf16[1024,2304]{1,0:T(8,128)(2,1)} %param.19), kind=kOutput, calls=%fused_computation.2 | convolution fusion | flops 4831838208 | bytes 11534336 | tf_op jit(solution)/shard_map/dot_general | solution.py:386
  59.2 0.0 copy-done.8
  59.2 10.4 %norm.1 = (bf16[1024,1024]{1,0:T(8,128)(2,1)S(1)}, bf16[1024,1024]{1,0:T(8,128)(2,1)}, f32[8,128,128]{2,1,0:T(8,128)S(1)}) custom-call(f32[1024,1024]{1,0:T(8,128)} %get-tuple-element.51.in_ref, bf16[1024,1024]{1,0:T(8,128)(2,1)S(1)} %copy-done.7, bf16[8,128,128]{2,1,0:T(8,128)(2,1)S(1)} %relay_forward.1.s_ref, bf16[1024,1024]{1,0:T(8,128)(2,1)} %fusion.up_ref, ...), custom_call_target="tpu_custom_call" | custom-call | tf_op jit(solution)/shard_map/norm/pallas_call | solution.py:391
  69.6 1.3 copy-done.3
  71.0 28.4 %prepare.2 = (bf16[1024,1024]{1,0:T(8,128)(2,1)}, bf16[1024,1024]{1,0:T(8,128)(2,1)S(1)}, bf16[16,8,128,128]{3,2,1,0:T(8,128)(2,1)}, bf16[1024,1024]{1,0:T(8,128...) custom-call(s32[2]{0:T(128)S(1)} %get-tuple-element.103.span, ...), custom_call_target="tpu_custom_call" | custom-call | tf_op jit(solution)/shard_map/prepare/pallas_call | solution.py:428
  99.4 20.2 %relay_back.1.ds_ref = bf16[8,128,128]{2,1,0:T(8,128)(2,1)S(1)} custom-call(f32[8,256,128]{2,1,0:T(8,128)S(1)} %get-tuple-element.53.map_ref.add_ref, f32[8,128,128]{2,1,0:T(8,128)S(1)} %get-tuple-element.73.add_ref), custom_call_target="tpu_custom_call" | custom-call | tf_op jit(solution)/shard_map/relay_back/pallas_call | solution.py:325
  119.5 0.0 copy-start
  119.5 0.0 copy-start.1
  119.6 10.2 %prepare.3 = (bf16[1024,1024]{1,0:T(8,128)(2,1)}, bf16[1024,1024]{1,0:T(8,128)(2,1)S(1)}, bf16[16,8,128,128]{3,2,1,0:T(8,128)(2,1)}, bf16[1024,1024]{1,0:T(8,128...) custom-call(s32[2]{0:T(128)S(1)} %get-tuple-element.102.span, ...), custom_call_target="tpu_custom_call", output_to_operand_aliasing={{0}: (10, {}), {1}: (11, {}), {2}: (12, {}), {3}: (13, {}),... | custom-call | tf_op jit(solution)/shard_map/prepare/pallas_call | solution.py:428
  129.7 1.3 copy-done.4
  131.1 1.3 copy-done.5
  132.4 0.0 copy-done.1
  132.4 24.3 %grad.1 = (bf16[1024,1024]{1,0:T(8,128)(2,1)}, bf16[1024,1024]{1,0:T(8,128)(2,1)}, f32[1024,1024]{1,0:T(8,128)}, f32[1024,8]{1,0:T(8,128)S(1)}) custom-call(s32[1]{0:T(128)S(6)} %copy.35.resets, bf16[1024,1024]{1,0:T(8,128)(2,1)S(1)} %copy-done, f32[1024,1024]{1,0:T(8,128)} %g_ref.7, f32[1024,8]{1,0:T(8,128)S(1)} %bitcast.9, f32[16,64,512]{2,1,0:T(8,128)S(1)} %copy-done.1, ...), custom_call_target="tpu_custom_call" | custom-call | tf_op jit(solution)/shard_map/grad/pallas_call | solution.py:464
  156.8 0.8 copy.26
  (8 shorter events, 0.0 us)
Async XLA Ops:
  7.2 42.6 %all-gather.2.cloned.1.call-start = ((), (), s32[]{:S(2)}) async-start(), calls=%async_computation | async-start | bytes 5898240 | tf_op jit(solution)/shard_map/all_gather | solution.py:349
  9.5 1.6 copy-start.2
  33.2 1.3 copy-start.6
  43.5 15.7 %copy-start.8 = (f32[128]{0:T(128)S(1)}, f32[128]{0:T(128)}, u32[]{:S(2)}) copy-start(f32[128]{0:T(128)} %param.18) | copy-start | bytes 1540
  49.7 9.5 %copy-start.7 = (bf16[1024,1024]{1,0:T(8,128)(2,1)S(1)}, bf16[1024,1024]{1,0:T(8,128)(2,1)}, u32[]{:S(2)}) copy-start(bf16[1024,1024]{1,0:T(8,128)(2,1)} %copy-done.6) | copy-start | bytes 6291460
  69.6 1.3 copy-start.3
  119.5 12.9 %copy-start = (bf16[1024,1024]{1,0:T(8,128)(2,1)S(1)}, bf16[1024,1024]{1,0:T(8,128)(2,1)}, u32[]{:S(2)}) copy-start(bf16[1024,1024]{1,0:T(8,128)(2,1)} %k_ref.7) | copy-start | bytes 6291460
  119.5 12.9 %copy-start.1 = (f32[16,64,512]{2,1,0:T(8,128)S(1)}, f32[16,64,512]{2,1,0:T(8,128)}, u32[]{:S(2)}) copy-start(f32[16,64,512]{2,1,0:T(8,128)} %w_ref.7) | copy-start | bytes 6291460
  129.7 1.3 copy-start.4
  131.1 1.3 copy-start.5
Sparse Core Ops, SparseCore 0:
  9.6 40.1 all-gather.1

commit v3 on v1

--- a/solution.py
+++ b/solution.py
@@ -12,7 +12,8 @@
 GROUP = 64
 SCALE = DK ** (-0.5)
 MESH = pl.DeviceIdType.MESH
-VMEM_LIMIT = 48 * 1024 * 1024
+VMEM_LIMIT = 63 * 1024 * 1024
+ROWS = 128
 f32 = jnp.float32
 bf16 = jnp.bfloat16
 
@@ -125,7 +126,9 @@
         total_ref[...] = state[...]
 
 
-def relay_kernel(n, forward, map_ref, add_ref, out_ref, arrive, depart, send_sem, recv_sem):
+def relay_kernel(
+    n, forward, map_ref, add_ref, out_ref, arrive, depart, parts, send_sem, recv_sem
+):
     me = lax.axis_index("seq")
     heads = out_ref.shape[0]
     if forward:
@@ -144,6 +147,12 @@
     @pl.when(has_target)
     def _():
         pl.semaphore_signal(barrier, inc=1, device_id={"seq": target}, device_id_type=MESH)
+
+    for h in range(heads):
+        matrix = map_ref[h, DV:]
+        high = matrix.astype(bf16)
+        rest = (matrix - high.astype(f32)).astype(bf16)
+        parts[h] = jnp.concatenate([high, rest], axis=0 if forward else 1)
 
     @pl.when(jnp.logical_and(me > 0, me < n - 1))
     def _():
@@ -166,23 +175,22 @@
 
     @pl.when(jnp.logical_not(has_source))
     def _():
-        out_ref[...] = jnp.zeros_like(out_ref)
+        arrive[...] = jnp.zeros_like(arrive)
 
     for h in range(heads):
         @pl.when(has_source)
         def _():
             copy(h).wait_recv()
-            out_ref[h] = arrive[h]
 
         @pl.when(has_target)
         def _():
-            matrix = map_ref[h, DV:]
-            high = matrix.astype(bf16)
-            rest = matrix - high.astype(f32)
-            now = out_ref[h]
-            times = nn if forward else nt
-            depart[h] = (add_ref[h, :DV] + (times(now, high) + times(now, rest))).astype(bf16)
+            now = arrive[h]
+            twice = jnp.concatenate([now, now], axis=1)
+            moved = nn(twice, parts[h]) if forward else nt(twice, parts[h])
+            depart[h] = (add_ref[h, :DV] + moved).astype(bf16)
             copy(h).start()
+
+    out_ref[...] = arrive[...]
 
     @pl.when(has_target)
     def _():
@@ -191,17 +199,18 @@
 
 
 def norm_kernel(in_ref, map_ref, s_ref, up_ref, gate_ref, gain_ref, go_ref, gg_ref, rest_ref):
-    maps = map_ref[...]
-    out = in_ref[...] + nt(maps, s_ref[0])
-    scale = lax.rsqrt(jnp.mean(out * out, axis=-1, keepdims=True) + 1e-06)
-    normal = out * scale
-    sig = jax.nn.sigmoid(gate_ref[...].astype(f32))
-    grad = up_ref[...] * gain_ref[...] * sig
-    gg_ref[...] = (grad * normal * (1.0 - sig)).astype(bf16)
-    inner = jnp.mean(grad * normal, axis=-1, keepdims=True)
-    grad_out = (scale * (grad - normal * inner)).astype(bf16)
-    go_ref[...] = grad_out
-    rest_ref[0] = tn(grad_out, maps)
+    for first in range(0, in_ref.shape[0], ROWS):
+        at = slice(first, first + ROWS)
+        out = in_ref[at] + nt(map_ref[at], s_ref[0])
+        scale = lax.rsqrt(jnp.mean(out * out, axis=-1, keepdims=True) + 1e-06)
+        normal = out * scale
+        sig = jax.nn.sigmoid(gate_ref[at].astype(f32))
+        grad = up_ref[at].astype(f32) * gain_ref[...] * sig
+        product = grad * normal
+        gg_ref[at] = (product * (1.0 - sig)).astype(bf16)
+        inner = jnp.mean(product, axis=-1, keepdims=True)
+        go_ref[at] = (scale * (grad - normal * inner)).astype(bf16)
+    rest_ref[0] = tn(go_ref[...], map_ref[...])
 
 
 def grad_kernel(
@@ -297,6 +306,7 @@
         scratch_shapes=[
             pltpu.VMEM((heads, DV, DK), bf16),
             pltpu.VMEM((heads, DV, DK), bf16),
+            pltpu.VMEM((heads, 2 * DK, DK) if forward else (heads, DK, 2 * DK), bf16),
             pltpu.SemaphoreType.DMA((heads,)),
             pltpu.SemaphoreType.DMA((heads,)),
         ],
@@ -312,7 +322,7 @@
     tokens, width = queries.shape
     heads = beta.shape[0]
     count = tokens // GROUP
-    together = 4 if heads % 4 == 0 else 1
+    together = heads
     gathered = lax.all_gather(grad_out, "head", axis=1, tiled=True)
     beta_rows = beta.T
 
@@ -351,7 +361,7 @@
     state_in = relay(n, True, total, total)
 
     upstream = lax.dot_general(
-        gathered, out_proj, (((1,), (1,)), ((), ())), preferred_element_type=f32
+        gathered, out_proj, (((1,), (1,)), ((), ())), preferred_element_type=bf16
     )
     column = pl.BlockSpec((tokens, DV), lambda h: (0, h))
     square = pl.BlockSpec((1, DV, DK), lambda h: (h, 0, 0))

time: 163 us -> 155 us (0.951)
  Pallas kernels: 128 us -> 121 us
  local copies, waits for them, and re-layouts: 6.03 us -> 3.61 us
  waiting for transfers between devices: 3.84 us -> 5.71 us
    pallas_call x1, Pallas kernels: 39 us -> 31.9 us  [per_device(): pl.pallas_call(functools.partial(grad_kernel, heads, together), grid=(cou...]
    unnamed x16 -> x2, local copies, waits for them, and re-layouts: 6.03 us -> 3.61 us
    pallas_call x2, Pallas kernels: 52.6 us -> 54.9 us  [relay(): pl.pallas_call(functools.partial(relay_kernel, n, forward), out_shape=jax...]
    pallas_call x1, Pallas kernels: 25.3 us -> 23.3 us  [per_device(): pl.pallas_call(functools.partial(local_kernel, heads, together), grid=(co...]
    all_gather x1, waiting for transfers between devices: 3.16 us -> 5.03 us  [per_device(): gathered = lax.all_gather(grad_out, 'head', axis=1, tiled=True)]
  transfers between devices with their start and end apart: 1 -> 1, of which waited for: 1 -> 1; matrix products, arithmetic and copies ran while one was open for 1% -> 1% of each run, Pallas kernels for 21% -> 22%
where the time goes in v3:
time: 155 us; the launch traced here: 154 us
  Pallas kernels  121 us (78%)
  between operations  14.7 us (9%)
  matrix products  9.35 us (6%)
  waiting for transfers between devices  5.71 us (4%)
  local copies, waits for them, and re-layouts  3.61 us (2%)
    pallas_call x2, Pallas kernels, relay(): pl.pallas_call(functools.partial(relay_kernel, n, forward), out_shape=jax...  54.9 us
    pallas_call x1, Pallas kernels, per_device(): pl.pallas_call(functools.partial(grad_kernel, heads, together), grid=(cou...  31.9 us
    pallas_call x1, Pallas kernels, per_device(): pl.pallas_call(functools.partial(local_kernel, heads, together), grid=(co...  23.3 us
    pallas_call x1, Pallas kernels, per_device(): pl.pallas_call(norm_kernel, grid=(heads,), in_specs=[column, column, squa...  10.5 us
    dot_general x1, matrix products, per_device(): lax.dot_general(gathered, out_proj, (((1,), (1,)), ((), ())), preferred_e...  9.35 us
    all_gather x1, waiting for transfers between devices, per_device(): gathered = lax.all_gather(grad_out, 'head', axis=1, tiled=True)  5.03 us
    unnamed x2, local copies, waits for them, and re-layouts  3.61 us
  transfers between devices with their start and end apart: 1, of which 1 were waited for; matrix products, arithmetic and copies ran while one was open for 1% of the time, Pallas kernels for 22%

profile of v3, /device:TPU:0, one launch (start us, length us, event | category | flops | bytes accessed | tf_op | source)
XLA Modules:
  0.0 154.1 jit_solution(10453767415336657917)
XLA Ops:
  7.2 0.0 all-gather.2.cloned.1.call-start
  7.2 0.7 all-gather.2.cloned.1.call-update
  8.5 1.8 %copy.17 = f32[8,1024]{0,1:T(8,128)} copy(f32[8,1024]{1,0:T(8,128)} %param.15) | data formatting | bytes 65536 | tf_op args[4]
  10.3 23.3 %local.1 = (f32[1024,1024]{1,0:T(8,128)}, bf16[1024,1024]{1,0:T(8,128)(2,1)}, bf16[16,8,256,128]{3,2,1,0:T(8,128)(2,1)}, f32[8,256,128]{2,1,0:T(8,128)}) custom-call(s32[1]{0:T(128)S(6)} %copy.19.resets, bf16[1024,1024]{1,0:T(8,128)(2,1)} %q_ref.3, bf16[1024,1024]{1,0:T(8,128)(2,1)} %k_ref.3, bf16[1024,1024]{1,0:T(8,128)(2,1)} %v_ref.3, f32[1024,1024]{1,0:T(8,128)} %g_ref.3, ...), custom_call_target="tpu_custom_call" | custom-call | tf_op jit(solution)/shard_map/local/pallas_call | solution.py:337
  33.7 11.0 %relay_forward.1.s_ref = bf16[8,128,128]{2,1,0:T(8,128)(2,1)} custom-call(f32[8,256,128]{2,1,0:T(8,128)} %get-tuple-element.20.map_ref.add_ref, f32[8,256,128]{2,1,0:T(8,128)} %get-tuple-element.20.map_ref.add_ref), custom_call_target="tpu_custom_call" | custom-call | tf_op jit(solution)/shard_map/relay_forward/pallas_call | solution.py:301
  44.7 5.0 %all-gather.2.cloned.1.call-done = bf16[1024,2304]{0,1:T(8,128)(2,1)} async-done(((bf16[1024,576]{0,1:T(8,128)(2,1)}), bf16[1024,2304]{0,1:T(8,128)(2,1)}) %all-gather.2.cloned.1.call-update) | async-done | bytes 4718608 | tf_op jit(solution)/shard_map/all_gather | solution.py:326
  49.7 9.4 %fusion.up_ref = bf16[1024,1024]{1,0:T(8,128)(2,1)} fusion(bf16[1024,2304]{0,1:T(8,128)(2,1)} %all-gather.2.cloned.1.call-done, bf16[1024,2304]{1,0:T(8,128)(2,1)} %param.19), kind=kOutput, calls=%fused_computation | convolution fusion | flops 4831838208 | bytes 11534336 | tf_op jit(solution)/shard_map/dot_general | solution.py:363
  59.1 10.5 %norm.1 = (bf16[1024,1024]{1,0:T(8,128)(2,1)}, bf16[1024,1024]{1,0:T(8,128)(2,1)}, f32[8,128,128]{2,1,0:T(8,128)}) custom-call(f32[1024,1024]{1,0:T(8,128)} %get-tuple-element.18.in_ref, bf16[1024,1024]{1,0:T(8,128)(2,1)} %get-tuple-element.19.map_ref, bf16[8,128,128]{2,1,0:T(8,128)(2,1)} %relay_forward.1.s_ref, bf16[1024,1024]{1,0:T(8,128)(2,1)} %fusion.up_ref, ...), custom_call_target="tpu_custom_call" | custom-call | tf_op jit(solution)/shard_map/norm/pallas_call | solution.py:368
  69.6 43.9 %relay_back.1.ds_ref = bf16[8,128,128]{2,1,0:T(8,128)(2,1)} custom-call(f32[8,256,128]{2,1,0:T(8,128)} %get-tuple-element.20.map_ref.add_ref, f32[8,128,128]{2,1,0:T(8,128)} %get-tuple-element.23.add_ref), custom_call_target="tpu_custom_call" | custom-call | tf_op jit(solution)/shard_map/relay_back/pallas_call | solution.py:301
  113.5 31.9 %grad.1 = (bf16[1024,1024]{1,0:T(8,128)(2,1)}, bf16[1024,1024]{1,0:T(8,128)(2,1)}, bf16[1024,1024]{1,0:T(8,128)(2,1)}, f32[1024,1024]{1,0:T(8,128)}, f32[1024,8]{1,0:T(8,128)}) custom-call(s32[1]{0:T(128)S(6)} %copy.19.resets, bf16[1024,1024]{1,0:T(8,128)(2,1)} %q_ref.3, bf16[1024,1024]{1,0:T(8,128)(2,1)} %k_ref.3, bf16[1024,1024]{1,0:T(8,128)(2,1)} %v_ref.3, ...), custom_call_target="tpu_custom_call" | custom-call | tf_op jit(solution)/shard_map/grad/pallas_call | solution.py:390
  145.4 1.8 %copy.18 = f32[8,1024]{1,0:T(8,128)} copy(f32[8,1024]{0,1:T(8,128)} %bitcast.7) | data formatting | bytes 65536
Async XLA Ops:
  7.2 42.6 %all-gather.2.cloned.1.call-start = ((), (), s32[]{:S(2)}) async-start(), calls=%async_computation | async-start | bytes 5898240 | tf_op jit(solution)/shard_map/all_gather | solution.py:326
Sparse Core Ops, SparseCore 0:
  9.6 40.1 all-gather.1

commit v4 on v3

--- a/solution.py
+++ b/solution.py
@@ -70,7 +70,7 @@
 
 def local_kernel(
     heads, together, resets, q_ref, k_ref, v_ref, g_ref, b_ref, w_ref,
-    out_ref, map_ref, enter_ref, total_ref, state,
+    out_ref, map_ref, enter_ref, offset_ref, matrix_ref, state,
 ):
     step = pl.program_id(0)
 
@@ -123,7 +123,9 @@
 
     @pl.when(step == pl.num_programs(0) - 1)
     def _():
-        total_ref[...] = state[...]
+        for h in range(heads):
+            offset_ref[h] = state[h, :DV]
+            matrix_ref[h] = state[h, DV:]
 
 
 def relay_kernel(
@@ -149,7 +151,7 @@
         pl.semaphore_signal(barrier, inc=1, device_id={"seq": target}, device_id_type=MESH)
 
     for h in range(heads):
-        matrix = map_ref[h, DV:]
+        matrix = map_ref[h]
         high = matrix.astype(bf16)
         rest = (matrix - high.astype(f32)).astype(bf16)
         parts[h] = jnp.concatenate([high, rest], axis=0 if forward else 1)
@@ -187,7 +189,7 @@
             now = arrive[h]
             twice = jnp.concatenate([now, now], axis=1)
             moved = nn(twice, parts[h]) if forward else nt(twice, parts[h])
-            depart[h] = (add_ref[h, :DV] + moved).astype(bf16)
+            depart[h] = (add_ref[h] + moved).astype(bf16)
             copy(h).start()
 
     out_ref[...] = arrive[...]
@@ -334,7 +336,7 @@
 
     scalar = pl.BlockSpec(memory_space=pltpu.SMEM)
     tile = pl.BlockSpec((GROUP, width), rows)
-    out_local, maps, enter, total = pl.pallas_call(
+    out_local, maps, enter, offset, matrix = pl.pallas_call(
         functools.partial(local_kernel, heads, together),
         grid=(count,),
         in_specs=[
@@ -345,20 +347,22 @@
         out_specs=[
             tile, tile,
             pl.BlockSpec((1, heads, DV + DK, DK), lambda i: (i, 0, 0, 0)),
-            pl.BlockSpec((heads, DV + DK, DK), lambda i: (0, 0, 0)),
+            pl.BlockSpec((heads, DV, DK), lambda i: (0, 0, 0)),
+            pl.BlockSpec((heads, DK, DK), lambda i: (0, 0, 0)),
         ],
         out_shape=[
             jax.ShapeDtypeStruct((tokens, width), f32),
             jax.ShapeDtypeStruct((tokens, width), bf16),
             jax.ShapeDtypeStruct((count, heads, DV + DK, DK), bf16),
-            jax.ShapeDtypeStruct((heads, DV + DK, DK), f32),
+            jax.ShapeDtypeStruct((heads, DV, DK), f32),
+            jax.ShapeDtypeStruct((heads, DK, DK), f32),
         ],
         scratch_shapes=[pltpu.VMEM((heads, DV + DK, DK), f32)],
         compiler_params=params(),
         name="local",
     )(resets, queries, keys, values, decay, beta_rows, wy_inverse)
 
-    state_in = relay(n, True, total, total)
+    state_in = relay(n, True, matrix, offset)
 
     upstream = lax.dot_general(
         gathered, out_proj, (((1,), (1,)), ((), ())), preferred_element_type=bf16
@@ -382,7 +386,7 @@
         name="norm",
     )(out_local, maps, state_in, upstream, out_gate, norm_gain.reshape(1, DV))
 
-    state_grad = relay(n, False, total, rest)
+    state_grad = relay(n, False, matrix, rest)
 
     tile = pl.BlockSpec((GROUP, width), rows_back)
     whole = pl.BlockSpec((heads, DV, DK), lambda i: (0, 0, 0))

time: 155 us -> 155 us (level)
  no operation moved by 1% of the time
where the time goes in v4:
time: 155 us; the launch traced here: 154 us
  Pallas kernels  120 us (77%)
  between operations  14.7 us (9%)
  matrix products  9.35 us (6%)
  waiting for transfers between devices  6.02 us (4%)
  local copies, waits for them, and re-layouts  3.61 us (2%)
    pallas_call x2, Pallas kernels, relay(): pl.pallas_call(functools.partial(relay_kernel, n, forward), out_shape=jax...  54.2 us
    pallas_call x1, Pallas kernels, per_device(): pl.pallas_call(functools.partial(grad_kernel, heads, together), grid=(cou...  31.9 us
    pallas_call x1, Pallas kernels, per_device(): pl.pallas_call(functools.partial(local_kernel, heads, together), grid=(co...  23.3 us
    pallas_call x1, Pallas kernels, per_device(): pl.pallas_call(norm_kernel, grid=(heads,), in_specs=[column, column, squa...  10.5 us
    dot_general x1, matrix products, per_device(): lax.dot_general(gathered, out_proj, (((1,), (1,)), ((), ())), preferred_e...  9.35 us
    all_gather x1, waiting for transfers between devices, per_device(): gathered = lax.all_gather(grad_out, 'head', axis=1, tiled=True)  5.34 us
    unnamed x2, local copies, waits for them, and re-layouts  3.61 us
  transfers between devices with their start and end apart: 1, of which 1 were waited for; matrix products, arithmetic and copies ran while one was open for 1% of the time, Pallas kernels for 22%

profile of v4, /device:TPU:0, one launch (start us, length us, event | category | flops | bytes accessed | tf_op | source)
XLA Modules:
  0.0 153.7 jit_solution(11349599593115677151)
XLA Ops:
  7.2 0.0 all-gather.2.cloned.1.call-start
  7.2 0.7 all-gather.2.cloned.1.call-update
  8.5 1.8 %copy.17 = f32[8,1024]{0,1:T(8,128)} copy(f32[8,1024]{1,0:T(8,128)} %param.15) | data formatting | bytes 65536 | tf_op args[4]
  10.3 23.3 %local.1 = (f32[1024,1024]{1,0:T(8,128)}, bf16[1024,1024]{1,0:T(8,128)(2,1)}, bf16[16,8,256,128]{3,2,1,0:T(8,128)(2,1)}, f32[8,128,128]{2,1,0:T(8,128)}, f32[8,128,128]{2,1,0:T(8,128)}) custom-call(s32[1]{0:T(128)S(6)} %copy.19.resets, bf16[1024,1024]{1,0:T(8,128)(2,1)} %q_ref.3, bf16[1024,1024]{1,0:T(8,128)(2,1)} %k_ref.3, bf16[1024,1024]{1,0:T(8,128)(2,1)} %v_ref.3, ...), custom_call_target="tpu_custom_call" | custom-call | tf_op jit(solution)/shard_map/local/pallas_call | solution.py:339
  33.7 10.7 %relay_forward.1.s_ref = bf16[8,128,128]{2,1,0:T(8,128)(2,1)} custom-call(f32[8,128,128]{2,1,0:T(8,128)} %get-tuple-element.21.map_ref, f32[8,128,128]{2,1,0:T(8,128)} %get-tuple-element.22.add_ref), custom_call_target="tpu_custom_call" | custom-call | tf_op jit(solution)/shard_map/relay_forward/pallas_call | solution.py:303
  44.4 5.3 %all-gather.2.cloned.1.call-done = bf16[1024,2304]{0,1:T(8,128)(2,1)} async-done(((bf16[1024,576]{0,1:T(8,128)(2,1)}), bf16[1024,2304]{0,1:T(8,128)(2,1)}) %all-gather.2.cloned.1.call-update) | async-done | bytes 4718608 | tf_op jit(solution)/shard_map/all_gather | solution.py:328
  49.7 9.4 %fusion.up_ref = bf16[1024,1024]{1,0:T(8,128)(2,1)} fusion(bf16[1024,2304]{0,1:T(8,128)(2,1)} %all-gather.2.cloned.1.call-done, bf16[1024,2304]{1,0:T(8,128)(2,1)} %param.19), kind=kOutput, calls=%fused_computation | convolution fusion | flops 4831838208 | bytes 11534336 | tf_op jit(solution)/shard_map/dot_general | solution.py:367
  59.1 10.5 %norm.1 = (bf16[1024,1024]{1,0:T(8,128)(2,1)}, bf16[1024,1024]{1,0:T(8,128)(2,1)}, f32[8,128,128]{2,1,0:T(8,128)}) custom-call(f32[1024,1024]{1,0:T(8,128)} %get-tuple-element.19.in_ref, bf16[1024,1024]{1,0:T(8,128)(2,1)} %get-tuple-element.20.map_ref, bf16[8,128,128]{2,1,0:T(8,128)(2,1)} %relay_forward.1.s_ref, bf16[1024,1024]{1,0:T(8,128)(2,1)} %fusion.up_ref, ...), custom_call_target="tpu_custom_call" | custom-call | tf_op jit(solution)/shard_map/norm/pallas_call | solution.py:372
  69.6 43.4 %relay_back.1.ds_ref = bf16[8,128,128]{2,1,0:T(8,128)(2,1)} custom-call(f32[8,128,128]{2,1,0:T(8,128)} %get-tuple-element.21.map_ref, f32[8,128,128]{2,1,0:T(8,128)} %get-tuple-element.25.add_ref), custom_call_target="tpu_custom_call" | custom-call | tf_op jit(solution)/shard_map/relay_back/pallas_call | solution.py:303
  113.1 31.9 %grad.1 = (bf16[1024,1024]{1,0:T(8,128)(2,1)}, bf16[1024,1024]{1,0:T(8,128)(2,1)}, bf16[1024,1024]{1,0:T(8,128)(2,1)}, f32[1024,1024]{1,0:T(8,128)}, f32[1024,8]{1,0:T(8,128)}) custom-call(s32[1]{0:T(128)S(6)} %copy.19.resets, bf16[1024,1024]{1,0:T(8,128)(2,1)} %q_ref.3, bf16[1024,1024]{1,0:T(8,128)(2,1)} %k_ref.3, bf16[1024,1024]{1,0:T(8,128)(2,1)} %v_ref.3, ...), custom_call_target="tpu_custom_call" | custom-call | tf_op jit(solution)/shard_map/grad/pallas_call | solution.py:394
  145.0 1.8 %copy.18 = f32[8,1024]{1,0:T(8,128)} copy(f32[8,1024]{0,1:T(8,128)} %bitcast.7) | data formatting | bytes 65536
Async XLA Ops:
  7.2 42.6 %all-gather.2.cloned.1.call-start = ((), (), s32[]{:S(2)}) async-start(), calls=%async_computation | async-start | bytes 5898240 | tf_op jit(solution)/shard_map/all_gather | solution.py:328
Sparse Core Ops, SparseCore 0:
  9.6 40.1 all-gather.1
